TPU v7x, 32 devices: a whole 2x2x4 slice. The times are simulated.
32 devices in a mesh: theta: 8 (over z, y), rad: 4 (over x, core).
Axes of the slice: x: 2, y: 2, z: 4, core: 2. Of those that a mesh axis runs over, the one named last changes fastest.
Arguments:
- flow_state: float32 [5, 7, 32, 32, 128], P(None, None, 'theta', 'rad'), may hold values from -6 to 16, as said below
- face_scale: float32 [32, 32, 128], P('theta', 'rad'), may hold values from 0.5 to 2
- volume: float32 [32, 32, 128], P('theta', 'rad'), may hold values from 0.5 to 2
- surface: float32 [9, 2048], P(None, ('theta', 'rad')), may hold values from -38 to 128, as said below
- centre_index: int32 [1024], P(('theta', 'rad')), may hold values from 0 to 2047, as said below
Outputs:
- residual: float32 [5, 7, 32, 32, 128], P(None, None, 'theta', 'rad')
Inputs may be any that keep to these rules, and one draw needn't show every extreme that they name: `flow_state`: row 0 (density) and the pressure 0.4 (row 4 - |rows 1 to 3|^2 / (2 row 0)) are positive everywhere. `surface`: the positions lie on the 12 blades between hub and shroud radius and within the axial extent of the grid; the displacement coefficients are at most 2.5 in magnitude. `centre_index`: the 32 entries held by one device are distinct and name nodes of that device's own block of 64 columns of surface.
All inputs are finite; a program needn't handle non-finite values.
Results may differ from a plain program's by a relative error of at most 0.0003.
Values sent between devices are 32-bit elements; how exact they have to be, the bound alone decides.
A program may use at most 64 MiB of HBM per device.

v0:
```python
import math

import jax
import jax.numpy as jnp
import numpy as np
from jax import lax
from jax.sharding import PartitionSpec as P

heat_ratio = 1.4
frequency = 0.8
damping = 0.0625
support_radius = 4.0
row_group = 4


def extended_2(value, sides, width, wrap):
    for axis, dim in sides:
        size, length = (lax.axis_size(axis), value.shape[dim])
        up = [(i, (i + 1) % size) for i in range(size if wrap else size - 1)]
        down = [(j, i) for i, j in up]
        last = lax.slice_in_dim(value, length - width, length, axis=dim)
        first = lax.slice_in_dim(value, 0, width, axis=dim)
        before = lax.ppermute(last, axis, up)
        after = lax.ppermute(first, axis, down)
        value = jnp.concatenate([before, value, after], axis=dim)
    return value


def derivative_table(instances):
    values = np.zeros((instances, instances))
    for row_index in range(instances):
        for col_index in range(instances):
            if row_index != col_index:
                steps_apart = row_index - col_index
                values[row_index, col_index] = (
                    0.5
                    * frequency
                    * (-1.0) ** steps_apart
                    / math.sin(math.pi * steps_apart / instances)
                )
    return values


def base_points(angular, radial, axial, theta_cells):
    hub_radius = theta_cells / (2.0 * math.pi)
    angle = 2.0 * math.pi / theta_cells * (angular.astype(jnp.float32) + 0.5)
    radius = hub_radius + radial.astype(jnp.float32) + 0.5
    height = axial.astype(jnp.float32) + 0.5
    return jnp.stack(
        jnp.broadcast_arrays(radius * jnp.cos(angle), radius * jnp.sin(angle), height), axis=0
    )


def rbf_harmonics(points, centres, scale):
    squared = jnp.zeros((centres.shape[1], points.shape[1]), jnp.float32)
    for component in range(3):
        squared = squared + (points[component][None, :] - centres[component][:, None]) ** 2
    kernel = 1.0 / jnp.sqrt(1.0 + squared / (scale * scale))
    return jnp.dot(
        centres[3:], kernel, precision=lax.Precision.HIGHEST, preferred_element_type=jnp.float32
    )


def deformation(harmonics, base, derivative):
    instances = derivative.shape[0]
    phases = 2.0 * math.pi * np.arange(instances) / instances
    extra = (1,) * (harmonics.ndim - 1)
    cosine = jnp.asarray(np.cos(phases), jnp.float32).reshape((1, instances) + extra)
    sine = jnp.asarray(np.sin(phases), jnp.float32).reshape((1, instances) + extra)
    shift = harmonics[:3, None] * cosine + harmonics[3:, None] * sine
    coords = base[:, None] + shift
    velocity = jnp.einsum("nm,cm...->cn...", derivative, shift, precision=lax.Precision.HIGHEST)
    return (coords, velocity)


def extend_edge(values, dim_index, layers):
    length = values.shape[dim_index]
    first_layer = lax.slice_in_dim(values, 0, 1, axis=dim_index)
    last_layer = lax.slice_in_dim(values, length - 1, length, axis=dim_index)
    return jnp.concatenate(
        [first_layer] * layers + [values] + [last_layer] * layers, axis=dim_index
    )


def extend_line(values, dim_index):
    length = values.shape[dim_index]
    first_layer = lax.slice_in_dim(values, 0, 1, axis=dim_index)
    second_layer = lax.slice_in_dim(values, 1, 2, axis=dim_index)
    last_layer = lax.slice_in_dim(values, length - 1, length, axis=dim_index)
    before_last = lax.slice_in_dim(values, length - 2, length - 1, axis=dim_index)
    return jnp.concatenate(
        [2.0 * first_layer - second_layer, values, 2.0 * last_layer - before_last], axis=dim_index
    )


def mend_edges(extended, layers, dim_index, at_first, at_last, linear):
    length = extended.shape[dim_index]
    inner_low = lax.slice_in_dim(extended, layers, layers + 1, axis=dim_index)
    inner_high = lax.slice_in_dim(extended, length - layers - 1, length - layers, axis=dim_index)
    if linear:
        next_low = lax.slice_in_dim(extended, layers + 1, layers + 2, axis=dim_index)
        next_high = lax.slice_in_dim(
            extended, length - layers - 2, length - layers - 1, axis=dim_index
        )
        inner_low = 2.0 * inner_low - next_low
        inner_high = 2.0 * inner_high - next_high
    low_fill = jnp.concatenate([inner_low] * layers, axis=dim_index)
    high_fill = jnp.concatenate([inner_high] * layers, axis=dim_index)
    old_low = lax.slice_in_dim(extended, 0, layers, axis=dim_index)
    old_high = lax.slice_in_dim(extended, length - layers, length, axis=dim_index)
    middle = lax.slice_in_dim(extended, layers, length - layers, axis=dim_index)
    return jnp.concatenate(
        [jnp.where(at_first, low_fill, old_low), middle, jnp.where(at_last, high_fill, old_high)],
        axis=dim_index,
    )


def physical_flux(states, normal, grid_speed):
    density = states[0]
    momentum = states[1:4]
    speed = momentum / density
    pressure = (heat_ratio - 1.0) * (states[4] - 0.5 * jnp.sum(momentum * speed, axis=0))
    relative = jnp.sum((speed - grid_speed) * normal, axis=0)
    return jnp.stack(
        [
            density * relative,
            momentum[0] * relative + pressure * normal[0],
            momentum[1] * relative + pressure * normal[1],
            momentum[2] * relative + pressure * normal[2],
            states[4] * relative + pressure * jnp.sum(speed * normal, axis=0),
        ],
        axis=0,
    )


def face_fluxes(states, coords, velocity, scales, dim_index):
    faces = coords.shape[dim_index] - 1

    def face_slice(values, offset, where_dim):
        return lax.slice_in_dim(values, offset, offset + faces, axis=where_dim)

    spacing = face_slice(coords, 1, dim_index) - face_slice(coords, 0, dim_index)
    length = jnp.sqrt(jnp.sum(spacing * spacing, axis=0))
    face_area = 0.5 * (face_slice(scales, 0, dim_index - 1) + face_slice(scales, 1, dim_index - 1))
    normal = spacing * (face_area / length)
    grid_speed = 0.5 * (face_slice(velocity, 0, dim_index) + face_slice(velocity, 1, dim_index))
    far_left = face_slice(states, 0, dim_index)
    left_state = face_slice(states, 1, dim_index)
    right_state = face_slice(states, 2, dim_index)
    far_right = face_slice(states, 3, dim_index)
    central = 0.5 * (
        physical_flux(left_state, normal, grid_speed)
        + physical_flux(right_state, normal, grid_speed)
    )
    average = 0.5 * (left_state + right_state)
    mean_speed = average[1:4] / average[0]
    mean_pressure = (heat_ratio - 1.0) * (
        average[4] - 0.5 * jnp.sum(average[1:4] * mean_speed, axis=0)
    )
    sound_speed = jnp.sqrt(heat_ratio * mean_pressure / average[0])
    spectral = (
        jnp.abs(jnp.sum((mean_speed - grid_speed) * normal, axis=0)) + sound_speed * face_area
    )
    return central + damping * spectral * (
        far_right - 3.0 * right_state + 3.0 * left_state - far_left
    )


def on_device(flow_state, face_scale, volume, surface, centre_index):
    variables, instances, theta_cells, radial_cells, axial_cells = flow_state.shape
    angular_count = lax.axis_size("theta")
    radial_count = lax.axis_size("rad")
    angular_pos = lax.axis_index("theta")
    radial_pos = lax.axis_index("rad")
    theta_total = theta_cells * angular_count
    derivative = jnp.asarray(derivative_table(instances), jnp.float32)
    node_count = surface.shape[1]
    own_ids = centre_index - (angular_pos * radial_count + radial_pos) * node_count
    payload = jnp.take(surface, own_ids, axis=1)
    angular = angular_pos * theta_cells + jnp.arange(theta_cells)
    radial = radial_pos * radial_cells + jnp.arange(radial_cells)
    axial = jnp.arange(axial_cells)
    interior = base_points(
        angular[:, None, None], radial[None, :, None], axial[None, None, :], theta_total
    )
    point_sets = interior.reshape(3, -1)
    block_size = row_group * axial_cells
    block_count = point_sets.shape[1] // block_size
    blocked = jnp.moveaxis(point_sets.reshape(3, block_count, block_size), 1, 0)
    portion = lax.all_gather(payload, ("theta", "rad"), axis=1, tiled=True)
    harmonics = jnp.zeros((block_count, 6, block_size), jnp.float32) + lax.map(
        lambda block: rbf_harmonics(block, portion, support_radius), blocked
    )
    harmonics = jnp.moveaxis(harmonics, 0, 1).reshape(6, -1)
    interior_count = theta_cells * radial_cells * axial_cells
    coords, velocity = deformation(
        harmonics[:, :interior_count].reshape(6, theta_cells, radial_cells, axial_cells),
        interior,
        derivative,
    )
    geometry_parts = [face_scale[None]]
    geometry_parts = geometry_parts + [
        coords.reshape(3 * instances, theta_cells, radial_cells, axial_cells),
        velocity.reshape(3 * instances, theta_cells, radial_cells, axial_cells),
    ]
    geometry_pack = jnp.concatenate(geometry_parts, axis=0)
    state_pack = flow_state.reshape(variables * instances, theta_cells, radial_cells, axial_cells)
    state_theta = extended_2(state_pack, (("theta", 1),), 2, True)
    state_rad = extended_2(state_pack, (("rad", 2),), 2, False)
    geometry_theta = extended_2(geometry_pack, (("theta", 1),), 1, True)
    geometry_rad = extended_2(geometry_pack, (("rad", 2),), 1, False)
    at_first = radial_pos == 0
    at_last = radial_pos == radial_count - 1
    state_theta = state_theta.reshape(
        variables, instances, theta_cells + 4, radial_cells, axial_cells
    )
    state_rad = mend_edges(state_rad, 2, 2, at_first, at_last, False).reshape(
        variables, instances, theta_cells, radial_cells + 4, axial_cells
    )
    scale_theta = geometry_theta[0:1]
    scale_rad = mend_edges(geometry_rad[0:1], 1, 2, at_first, at_last, False)
    split_at = 1 + 3 * instances
    coords_theta = geometry_theta[1:split_at].reshape(
        3, instances, theta_cells + 2, radial_cells, axial_cells
    )
    velocity_theta = geometry_theta[split_at:].reshape(
        3, instances, theta_cells + 2, radial_cells, axial_cells
    )
    coords_rad = geometry_rad[1:split_at].reshape(
        3, instances, theta_cells, radial_cells + 2, axial_cells
    )
    velocity_rad = geometry_rad[split_at:].reshape(
        3, instances, theta_cells, radial_cells + 2, axial_cells
    )
    coords_rad = mend_edges(coords_rad, 1, 3, at_first, at_last, True)
    velocity_rad = mend_edges(velocity_rad, 1, 3, at_first, at_last, False)
    state_axial = extend_edge(flow_state, 4, 2)
    coords_axial = extend_line(coords, 4)
    velocity_axial = extend_edge(velocity, 4, 1)
    scale_axial = extend_edge(face_scale[None], 3, 1)
    running = jnp.zeros_like(flow_state)
    directions = (
        (2, state_theta, coords_theta, velocity_theta, scale_theta),
        (3, state_rad, coords_rad, velocity_rad, scale_rad),
        (4, state_axial, coords_axial, velocity_axial, scale_axial),
    )
    for dim_index, ext_states, ext_coords, ext_velocity, ext_scales in directions:
        fluxes = face_fluxes(ext_states, ext_coords, ext_velocity, ext_scales, dim_index)
        faces = fluxes.shape[dim_index]
        running = (
            running
            + lax.slice_in_dim(fluxes, 1, faces, axis=dim_index)
            - lax.slice_in_dim(fluxes, 0, faces - 1, axis=dim_index)
        )
    temporal = jnp.einsum(
        "nm,vm...->vn...",
        derivative,
        volume[None, None] * flow_state,
        precision=lax.Precision.HIGHEST,
    )
    return temporal + running


def solution(mesh):
    return jax.shard_map(
        on_device,
        mesh=mesh,
        in_specs=(
            P(None, None, "theta", "rad", None),
            P("theta", "rad", None),
            P("theta", "rad", None),
            P(None, ("theta", "rad")),
            P(("theta", "rad")),
        ),
        out_specs=P(None, None, "theta", "rad", None),
        check_vma=False,
    )
```

profile of v0, /device:TPU:0, one launch (start us, length us, event | category | flops | bytes accessed | tf_op | source)
XLA Modules:
  0.0 113.3 jit_solution(10799162515586340550)
XLA Ops:
  2.6 43.9 %all-gather = f32[32,32,9]{1,2,0:T(8,128)S(1)} all-gather(f32[1,32,9]{1,2,0:T(8,128)S(1)} %copy.176), channel_id=1, replica_groups=mesh['theta'=8,'rad'=4] {'theta','rad'}, dimensions={0}, use_global_device_ids=true | all-gather | bytes 38016 | tf_op jit(solution)/shard_map/all_gather | solution.py:190
  46.7 16.3 %while.10 = (s32[]{:T(128)}, f32[8,6,512]{2,1,0:T(8,128)S(1)}, f32[8,3,512]{2,0,1:T(8,128)S(1)}, f32[9,1024]{1,0:T(8,128)S(1)}, s32[]{:T(128)}, /*index=5*/s32[]{:T(128)}, s32[]{}, s32[]{}) while((s32[]{:T(128)}, f32[8,6,512]{2,1,0:T(8,128)S(1)}, f32[8,3,512]{2,0,1:T(8,128)S(1)}, f32[9,1024]{1,0:T(8,128)S(1)}, s32[]{:T(128)}, ...), condition=%wide.region_1.2_spmd, body=%wide.region_0.1_spmd.sunk | while | flops 42991620 | bytes 104573 | solution.py:191
  46.7 2.0 %fusion.192 = f32[8,6,512]{2,1,0:T(8,128)S(1)} fusion(f32[8,6,512]{2,1,0:T(8,128)S(1)} %get-tuple-element.225, s32[]{:T(128)} %get-tuple-element.224, f32[1024]{0:T(1024)S(1)} %bitcast.292, f32[512]{0:T(512)S(1)} %bitcast.296, f32[1024]{0:T(1024)S(1)} %bitcast.293, f32[512]{0:T(512)S(1)} %bitcast.295, f32[1024]{0:T(1024)S(1)} %bitcast.291, ...), kind=kOutput, calls=%fused_computation.14.clone.1 | convolution fusion | flops 42991616 | bytes 67588 | tf_op jit(solution)/shard_map/while/body/eval_jaxpr/dot_general | solution.py:59
  48.8 2.0 %fusion.192 = f32[8,6,512]{2,1,0:T(8,128)S(1)} fusion(f32[8,6,512]{2,1,0:T(8,128)S(1)} %get-tuple-element.225, s32[]{:T(128)} %get-tuple-element.224, f32[1024]{0:T(1024)S(1)} %bitcast.292, f32[512]{0:T(512)S(1)} %bitcast.296, f32[1024]{0:T(1024)S(1)} %bitcast.293, f32[512]{0:T(512)S(1)} %bitcast.295, f32[1024]{0:T(1024)S(1)} %bitcast.291, ...), kind=kOutput, calls=%fused_computation.14.clone.1 | convolution fusion | flops 42991616 | bytes 67588 | tf_op jit(solution)/shard_map/while/body/eval_jaxpr/dot_general | solution.py:59
  50.8 2.0 %fusion.192 = f32[8,6,512]{2,1,0:T(8,128)S(1)} fusion(f32[8,6,512]{2,1,0:T(8,128)S(1)} %get-tuple-element.225, s32[]{:T(128)} %get-tuple-element.224, f32[1024]{0:T(1024)S(1)} %bitcast.292, f32[512]{0:T(512)S(1)} %bitcast.296, f32[1024]{0:T(1024)S(1)} %bitcast.293, f32[512]{0:T(512)S(1)} %bitcast.295, f32[1024]{0:T(1024)S(1)} %bitcast.291, ...), kind=kOutput, calls=%fused_computation.14.clone.1 | convolution fusion | flops 42991616 | bytes 67588 | tf_op jit(solution)/shard_map/while/body/eval_jaxpr/dot_general | solution.py:59
  52.8 2.0 %fusion.192 = f32[8,6,512]{2,1,0:T(8,128)S(1)} fusion(f32[8,6,512]{2,1,0:T(8,128)S(1)} %get-tuple-element.225, s32[]{:T(128)} %get-tuple-element.224, f32[1024]{0:T(1024)S(1)} %bitcast.292, f32[512]{0:T(512)S(1)} %bitcast.296, f32[1024]{0:T(1024)S(1)} %bitcast.293, f32[512]{0:T(512)S(1)} %bitcast.295, f32[1024]{0:T(1024)S(1)} %bitcast.291, ...), kind=kOutput, calls=%fused_computation.14.clone.1 | convolution fusion | flops 42991616 | bytes 67588 | tf_op jit(solution)/shard_map/while/body/eval_jaxpr/dot_general | solution.py:59
  54.9 2.0 %fusion.192 = f32[8,6,512]{2,1,0:T(8,128)S(1)} fusion(f32[8,6,512]{2,1,0:T(8,128)S(1)} %get-tuple-element.225, s32[]{:T(128)} %get-tuple-element.224, f32[1024]{0:T(1024)S(1)} %bitcast.292, f32[512]{0:T(512)S(1)} %bitcast.296, f32[1024]{0:T(1024)S(1)} %bitcast.293, f32[512]{0:T(512)S(1)} %bitcast.295, f32[1024]{0:T(1024)S(1)} %bitcast.291, ...), kind=kOutput, calls=%fused_computation.14.clone.1 | convolution fusion | flops 42991616 | bytes 67588 | tf_op jit(solution)/shard_map/while/body/eval_jaxpr/dot_general | solution.py:59
  56.9 2.0 %fusion.192 = f32[8,6,512]{2,1,0:T(8,128)S(1)} fusion(f32[8,6,512]{2,1,0:T(8,128)S(1)} %get-tuple-element.225, s32[]{:T(128)} %get-tuple-element.224, f32[1024]{0:T(1024)S(1)} %bitcast.292, f32[512]{0:T(512)S(1)} %bitcast.296, f32[1024]{0:T(1024)S(1)} %bitcast.293, f32[512]{0:T(512)S(1)} %bitcast.295, f32[1024]{0:T(1024)S(1)} %bitcast.291, ...), kind=kOutput, calls=%fused_computation.14.clone.1 | convolution fusion | flops 42991616 | bytes 67588 | tf_op jit(solution)/shard_map/while/body/eval_jaxpr/dot_general | solution.py:59
  58.9 2.0 %fusion.192 = f32[8,6,512]{2,1,0:T(8,128)S(1)} fusion(f32[8,6,512]{2,1,0:T(8,128)S(1)} %get-tuple-element.225, s32[]{:T(128)} %get-tuple-element.224, f32[1024]{0:T(1024)S(1)} %bitcast.292, f32[512]{0:T(512)S(1)} %bitcast.296, f32[1024]{0:T(1024)S(1)} %bitcast.293, f32[512]{0:T(512)S(1)} %bitcast.295, f32[1024]{0:T(1024)S(1)} %bitcast.291, ...), kind=kOutput, calls=%fused_computation.14.clone.1 | convolution fusion | flops 42991616 | bytes 67588 | tf_op jit(solution)/shard_map/while/body/eval_jaxpr/dot_general | solution.py:59
  61.0 2.0 %fusion.192 = f32[8,6,512]{2,1,0:T(8,128)S(1)} fusion(f32[8,6,512]{2,1,0:T(8,128)S(1)} %get-tuple-element.225, s32[]{:T(128)} %get-tuple-element.224, f32[1024]{0:T(1024)S(1)} %bitcast.292, f32[512]{0:T(512)S(1)} %bitcast.296, f32[1024]{0:T(1024)S(1)} %bitcast.293, f32[512]{0:T(512)S(1)} %bitcast.295, f32[1024]{0:T(1024)S(1)} %bitcast.291, ...), kind=kOutput, calls=%fused_computation.14.clone.1 | convolution fusion | flops 42991616 | bytes 67588 | tf_op jit(solution)/shard_map/while/body/eval_jaxpr/dot_general | solution.py:59
  64.9 4.7 %collective-permute-start.2 = (f32[43,1,8,128]{3,2,1,0:T(8,128)}, f32[43,1,8,128]{3,2,1,0:T(8,128)}, u32[]{:S(2)}, u32[]{:S(2)}) collective-permute-start(f32[43,1,8,128]{3,2,1,0:T(8,128)} %get-tuple-element.109), channel_id=1, source_target_pairs={{4,0},{8,4},{12,8},{16,12},{20,16},{24,20},{28,24},{0,28},{5,1},{9... | collective-permute-start | bytes 528392 | tf_op jit(solution)/shard_map/ppermute | solution.py:24
  70.5 2.3 %collective-permute-start.4 = (f32[35,4,2,128]{3,2,1,0:T(2,128)}, f32[35,4,2,128]{3,2,1,0:T(2,128)}, u32[]{:S(2)}, u32[]{:S(2)}) collective-permute-start(f32[35,4,2,128]{3,2,1,0:T(2,128)} %get-tuple-element.130), channel_id=1, source_target_pairs={{0,1},{1,2},{2,3},{4,5},{5,6},{6,7},{8,9},{9,10},{10,11},{12,13},{... | collective-permute-start | bytes 430088 | tf_op jit(solution)/shard_map/ppermute | solution.py:23
  73.6 1.9 %collective-permute-start.5 = (f32[43,4,1,128]{3,2,1,0:T(1,128)}, f32[43,4,1,128]{3,2,1,0:T(1,128)}, u32[]{:S(2)}, u32[]{:S(2)}) collective-permute-start(f32[43,4,1,128]{3,2,1,0:T(1,128)} %get-tuple-element.110), channel_id=1, source_target_pairs={{0,1},{1,2},{2,3},{4,5},{5,6},{6,7},{8,9},{9,10},{10,11},{12,13},{... | collective-permute-start | bytes 264200 | tf_op jit(solution)/shard_map/ppermute | solution.py:23
  75.5 1.3 %collective-permute-start.6 = (f32[43,4,1,128]{3,2,1,0:T(1,128)}, f32[43,4,1,128]{3,2,1,0:T(1,128)}, u32[]{:S(2)}, u32[]{:S(2)}) collective-permute-start(f32[43,4,1,128]{3,2,1,0:T(1,128)} %get-tuple-element.111), channel_id=1, source_target_pairs={{1,0},{2,1},{3,2},{5,4},{6,5},{7,6},{9,8},{10,9},{11,10},{13,12},{... | collective-permute-start | bytes 264200 | tf_op jit(solution)/shard_map/ppermute | solution.py:24
  78.6 1.3 %slice_subtract_fusion.8 = (f32[3,7,4,8,1]{4,1,3,2,0:T(8,128)S(1)}, f32[3,7,4,8,1]{4,1,3,2,0:T(8,128)S(1)}, f32[3,7,4,8,1]{4,1,3,2,0:T(8,128)}, f32[3,7,4,8,1]{4,1,3,2,0:T(8,128)}) fusion(f32[3,7,4,8,128]{4,1,3,2,0:T(8,128)S(1)} %fusion.48, f32[3,7,4,8,128]{4,1,3,2,0:T(8,128)S(1)} %convolution_bitcast_fusion.1), kind=kLoop, calls=%fused_computation.144 | loop fusion | flops 2688 | bytes 26880 | tf_op jit(solution)/shard_map/sub | solution.py:92
  81.1 1.3 %collective-permute-start.7 = (f32[35,4,2,128]{3,2,1,0:T(2,128)}, f32[35,4,2,128]{3,2,1,0:T(2,128)S(1)}, u32[]{:S(2)}, u32[]{:S(2)}) collective-permute-start(f32[35,4,2,128]{3,2,1,0:T(2,128)} %get-tuple-element.129), channel_id=1, source_target_pairs={{1,0},{2,1},{3,2},{5,4},{6,5},{7,6},{9,8},{10,9},{11,10},{13,12},{... | collective-permute-start | bytes 430088 | tf_op jit(solution)/shard_map/ppermute | solution.py:24
  82.4 1.1 pad_maximum_fusion.6
  85.4 4.9 %collective-permute-start.3 = (f32[35,2,8,128]{3,2,1,0:T(8,128)S(1)}, f32[35,2,8,128]{3,2,1,0:T(8,128)S(1)}, u32[]{:S(2)}, u32[]{:S(2)}) collective-permute-start(f32[35,2,8,128]{3,2,1,0:T(8,128)S(1)} %copy-done.5), channel_id=1, source_target_pairs={{4,0},{8,4},{12,8},{16,12},{20,16},{24,20},{28,24},{0,28},{5,1},{9... | collective-permute-start | bytes 860168 | tf_op jit(solution)/shard_map/ppermute | solution.py:24
  90.7 1.1 pad_maximum_fusion.11
  92.9 2.2 %collective-permute-done = f32[35,2,8,128]{3,2,1,0:T(8,128)S(1)} collective-permute-done((f32[35,2,8,128]{3,2,1,0:T(8,128)}, f32[35,2,8,128]{3,2,1,0:T(8,128)S(1)}, u32[]{:S(2)}, u32[]{:S(2)}) %collective-permute-start) | collective-permute-done | bytes 286752 | tf_op jit(solution)/shard_map/ppermute | solution.py:23
  95.6 5.5 %collective-permute-done.3 = f32[35,2,8,128]{3,2,1,0:T(8,128)S(1)} collective-permute-done((f32[35,2,8,128]{3,2,1,0:T(8,128)S(1)}, f32[35,2,8,128]{3,2,1,0:T(8,128)S(1)}, u32[]{:S(2)}, u32[]{:S(2)}) %collective-permute-start.3) | collective-permute-done | bytes 286752 | tf_op jit(solution)/shard_map/ppermute | solution.py:24
  105.4 1.0 multiply_reduce_fusion.1
  109.4 1.6 %fusion.33 = f32[5,7,4,8,129]{4,1,3,2,0:T(8,128)S(1)} fusion(f32[5,7,4,8,1]{4,1,3,2,0:T(8,128)S(1)} %get-tuple-element.119, f32[5,7,4,8,1]{4,1,3,2,0:T(8,128)S(1)} %get-tuple-element.118, f32[5,7,4,8,128]{4,1,3,2,0:T(8,128)S(1)} %get-tuple-element.126, f32[5,7,4,8,129]{4,1,3,2,0:T(8,128)S(1)} %get-tuple-element.113, ...), kind=kLoop, calls=%fused_computation.61 | loop fusion | flops 2167200 | bytes 2431744 | tf_op jit(solution)/shard_map/add | solution.py:164
  111.0 1.3 %fusion.35 = f32[5,7,4,8,128]{4,1,3,2,0:T(8,128)S(1)} fusion(f32[7,7,1,1,1]{1,0,4,3,2:T(8,128)S(1)} %copy-done.8, f32[5,7,4,8,129]{4,1,3,2,0:T(8,128)S(1)} %fusion.33, f32[5,7,4,9,128]{4,1,3,2,0:T(8,128)S(1)} %fusion.43, f32[5,7,5,8,128]{4,1,3,2,0:T(8,128)S(1)} %fusion.37, f32[5,7,4,8,128]{4,3,2,1,0:T(8,128)S(1)} %broadcast_multiply_fusion.1), kind=kOutput, calls=%fused_computation.66 | convolution fusion | flops 12902400 | bytes 4587716 | tf_op jit(solution)/shard_map/nm,vm...->vn.../dot_general | solution.py:255
  (156 shorter events, 21.0 us)
Async XLA Ops:
  46.6 16.4 %copy-start.9 = (f32[7]{0:T(128)S(1)}, f32[7]{0:T(128)}, u32[]{:S(2)}) copy-start(f32[7]{0:T(128)} %constant.26.clone) | copy-start | bytes 88
  46.7 16.5 %copy-start.10 = (f32[7]{0:T(128)S(1)}, f32[7]{0:T(128)}, u32[]{:S(2)}) copy-start(f32[7]{0:T(128)} %constant.27.clone) | copy-start | bytes 88
  46.7 16.6 %copy-start.8 = (f32[7,7,1,1,1]{1,0,4,3,2:T(8,128)S(1)}, f32[7,7,1,1,1]{1,0,4,3,2:T(8,128)}, u32[]{:S(2)}) copy-start(f32[7,7,1,1,1]{1,0,4,3,2:T(8,128)} %constant.31) | copy-start | bytes 592
  63.0 1.1 copy-start.3
  63.9 5.7 %copy-start = (f32[5,7,4,8,128]{4,3,2,1,0:T(8,128)S(1)}, f32[5,7,4,8,128]{4,3,2,1,0:T(8,128)}, u32[]{:S(2)}) copy-start(f32[5,7,4,8,128]{4,3,2,1,0:T(8,128)} %param.10) | copy-start | bytes 1720324
  64.9 25.8 %collective-permute-start.1 = (f32[43,1,8,128]{3,2,1,0:T(8,128)}, f32[43,1,8,128]{3,2,1,0:T(8,128)}, u32[]{:S(2)}, u32[]{:S(2)}) collective-permute-start(f32[43,1,8,128]{3,2,1,0:T(8,128)} %get-tuple-element.108), channel_id=1, source_target_pairs={{0,4},{4,8},{8,12},{12,16},{16,20},{20,24},{24,28},{28,0},{1,5},{5... | collective-permute-start | bytes 528392 | tf_op jit(solution)/shard_map/ppermute | solution.py:23
  64.9 25.8 %collective-permute-start.2 = (f32[43,1,8,128]{3,2,1,0:T(8,128)}, f32[43,1,8,128]{3,2,1,0:T(8,128)}, u32[]{:S(2)}, u32[]{:S(2)}) collective-permute-start(f32[43,1,8,128]{3,2,1,0:T(8,128)} %get-tuple-element.109), channel_id=1, source_target_pairs={{4,0},{8,4},{12,8},{16,12},{20,16},{24,20},{28,24},{0,28},{5,1},{9... | collective-permute-start | bytes 528392 | tf_op jit(solution)/shard_map/ppermute | solution.py:24
  70.5 15.0 %collective-permute-start.4 = (f32[35,4,2,128]{3,2,1,0:T(2,128)}, f32[35,4,2,128]{3,2,1,0:T(2,128)}, u32[]{:S(2)}, u32[]{:S(2)}) collective-permute-start(f32[35,4,2,128]{3,2,1,0:T(2,128)} %get-tuple-element.130), channel_id=1, source_target_pairs={{0,1},{1,2},{2,3},{4,5},{5,6},{6,7},{8,9},{9,10},{10,11},{12,13},{... | collective-permute-start | bytes 430088 | tf_op jit(solution)/shard_map/ppermute | solution.py:23
  73.6 7.5 %collective-permute-start.5 = (f32[43,4,1,128]{3,2,1,0:T(1,128)}, f32[43,4,1,128]{3,2,1,0:T(1,128)}, u32[]{:S(2)}, u32[]{:S(2)}) collective-permute-start(f32[43,4,1,128]{3,2,1,0:T(1,128)} %get-tuple-element.110), channel_id=1, source_target_pairs={{0,1},{1,2},{2,3},{4,5},{5,6},{6,7},{8,9},{9,10},{10,11},{12,13},{... | collective-permute-start | bytes 264200 | tf_op jit(solution)/shard_map/ppermute | solution.py:23
  75.5 6.9 %collective-permute-start.6 = (f32[43,4,1,128]{3,2,1,0:T(1,128)}, f32[43,4,1,128]{3,2,1,0:T(1,128)}, u32[]{:S(2)}, u32[]{:S(2)}) collective-permute-start(f32[43,4,1,128]{3,2,1,0:T(1,128)} %get-tuple-element.111), channel_id=1, source_target_pairs={{1,0},{2,1},{3,2},{5,4},{6,5},{7,6},{9,8},{10,9},{11,10},{13,12},{... | collective-permute-start | bytes 264200 | tf_op jit(solution)/shard_map/ppermute | solution.py:24
  78.6 1.3 %copy-start.7 = (f32[4,8,128]{2,1,0:T(8,128)S(1)}, f32[4,8,128]{2,1,0:T(8,128)}, u32[]{:S(2)}) copy-start(f32[4,8,128]{2,1,0:T(8,128)} %param.12) | copy-start | bytes 49156
  81.1 9.3 %collective-permute-start.7 = (f32[35,4,2,128]{3,2,1,0:T(2,128)}, f32[35,4,2,128]{3,2,1,0:T(2,128)S(1)}, u32[]{:S(2)}, u32[]{:S(2)}) collective-permute-start(f32[35,4,2,128]{3,2,1,0:T(2,128)} %get-tuple-element.129), channel_id=1, source_target_pairs={{1,0},{2,1},{3,2},{5,4},{6,5},{7,6},{9,8},{10,9},{11,10},{13,12},{... | collective-permute-start | bytes 430088 | tf_op jit(solution)/shard_map/ppermute | solution.py:24
  82.4 12.7 %collective-permute-start = (f32[35,2,8,128]{3,2,1,0:T(8,128)}, f32[35,2,8,128]{3,2,1,0:T(8,128)S(1)}, u32[]{:S(2)}, u32[]{:S(2)}) collective-permute-start(f32[35,2,8,128]{3,2,1,0:T(8,128)} %get-tuple-element.121), channel_id=1, source_target_pairs={{0,4},{4,8},{8,12},{12,16},{16,20},{20,24},{24,28},{28,0},{1,5},{5... | collective-permute-start | bytes 860168 | tf_op jit(solution)/shard_map/ppermute | solution.py:23
  84.3 1.1 %copy-start.5 = (f32[35,2,8,128]{3,2,1,0:T(8,128)S(1)}, f32[35,2,8,128]{3,2,1,0:T(8,128)}, u32[]{:S(2)}) copy-start(f32[35,2,8,128]{3,2,1,0:T(8,128)} %get-tuple-element.120) | copy-start | bytes 860164
  84.3 6.1 %copy-start.6 = (f32[35,4,1,128]{3,2,1,0:T(1,128)S(1)}, f32[35,4,1,128]{3,2,1,0:T(1,128)}, u32[]{:S(2)}) copy-start(f32[35,4,1,128]{3,2,1,0:T(1,128)} %get-tuple-element.128) | copy-start | bytes 215044
  85.4 15.7 %collective-permute-start.3 = (f32[35,2,8,128]{3,2,1,0:T(8,128)S(1)}, f32[35,2,8,128]{3,2,1,0:T(8,128)S(1)}, u32[]{:S(2)}, u32[]{:S(2)}) collective-permute-start(f32[35,2,8,128]{3,2,1,0:T(8,128)S(1)} %copy-done.5), channel_id=1, source_target_pairs={{4,0},{8,4},{12,8},{16,12},{20,16},{24,20},{28,24},{0,28},{5,1},{9... | collective-permute-start | bytes 860168 | tf_op jit(solution)/shard_map/ppermute | solution.py:24
  104.2 1.0 copy-start.1
  104.2 1.1 copy-start.2
  104.2 1.2 %copy-start.4 = (f32[7,4,8,129]{3,0,2,1:T(8,128)S(1)}, f32[7,4,8,129]{3,0,2,1:T(8,128)}, u32[]{:S(2)}) copy-start(f32[7,4,8,129]{3,0,2,1:T(8,128)} %rsqrt_multiply_fusion) | copy-start | bytes 346756
where the time goes:
time: 114 us; the launch traced here: 113 us
  blocking collectives  43.9 us (39%)
  matrix products  17.9 us (16%)
  other arithmetic  17.3 us (15%)
  starting transfers between devices  16.5 us (14%)
  local copies, waits for them, and re-layouts  9.11 us (8%)
  waiting for transfers between devices  7.71 us (7%)
    all_gather x1, blocking collectives, on_device(): portion = lax.all_gather(payload, ('theta', 'rad'), axis=1, tiled=True)  43.9 us
    dot_general x8, matrix products, rbf_harmonics(): jnp.dot(centres[3:], kernel, precision=lax.Precision.HIGHEST, preferred_e...  16 us
    ppermute x4, starting transfers between devices, extended_2(): after = lax.ppermute(first, axis, down)  12.2 us
    ppermute x4, waiting for transfers between devices, extended_2(): after = lax.ppermute(first, axis, down)  5.54 us
    ppermute x4, starting transfers between devices, extended_2(): before = lax.ppermute(last, axis, up)  4.32 us
    unnamed x30, local copies, waits for them, and re-layouts  2.56 us
    add x3, other arithmetic, face_fluxes(): central + damping * spectral * (far_right - 3.0 * right_state + 3.0 * lef...  2.35 us
  transfers between devices with their start and end apart: 8, of which 2 were waited for; matrix products, arithmetic and copies ran while one was open for 10% of the time, Pallas kernels for 0%

commit v1 on v0

v1 whole, which is shorter than its diff:
```python
import functools
import math

import jax
import jax.numpy as jnp
import numpy as np
from jax import lax
from jax.experimental import pallas as pl
from jax.experimental.pallas import tpu as pltpu
from jax.sharding import PartitionSpec as P

heat_ratio = 1.4
frequency = 0.8
damping = 0.0625
support_radius = 4.0
LANES = 128
MESH = pl.DeviceIdType.MESH


def derivative_table(instances):
    values = np.zeros((instances, instances))
    for row in range(instances):
        for col in range(instances):
            if row != col:
                steps = row - col
                values[row, col] = (
                    0.5 * frequency * (-1.0) ** steps / math.sin(math.pi * steps / instances)
                )
    return values


def constant_rows(instances, theta_total):
    phases = 2.0 * math.pi * np.arange(instances) / instances
    derivative = derivative_table(instances)
    rows = []
    for values in (np.cos(phases), np.sin(phases)):
        rows.append(np.resize(values, 8))
    for values in (np.cos(phases), np.sin(phases)):
        rows.append(np.resize(derivative @ values, 8))
    angle = 2.0 * math.pi / theta_total * (np.arange(theta_total) + 0.5)
    rows.append(np.cos(angle))
    rows.append(np.sin(angle))
    column = np.concatenate(rows).astype(np.float32)
    return np.ascontiguousarray(np.broadcast_to(column[:, None], (column.size, LANES)))


def dot3(a, b):
    return a[0] * b[0] + a[1] * b[1] + a[2] * b[2]


def face_flux(left, right, prim_l, prim_r, third, spacing, speed_sum, scale_sum):
    area = 0.5 * scale_sum
    factor = (0.5 * area) * lax.rsqrt(dot3(spacing, spacing))
    half = [s * factor for s in spacing]
    grid = 0.5 * dot3(speed_sum, half)
    un_l = dot3(prim_l, half)
    un_r = dot3(prim_r, half)
    q_l, q_r = un_l - grid, un_r - grid
    pressure = prim_l[3] + prim_r[3]
    flux = [left[v] * q_l + right[v] * q_r for v in range(5)]
    for c in range(3):
        flux[1 + c] = flux[1 + c] + pressure * half[c]
    flux[4] = flux[4] + prim_l[3] * un_l + prim_r[3] * un_r
    total = [left[v] + right[v] for v in range(5)]
    inverse = 1.0 / total[0]
    mean = [total[1 + c] * inverse for c in range(3)]
    sound2 = (heat_ratio * (heat_ratio - 1.0)) * (
        (total[4] - 0.5 * dot3(total[1:4], mean)) * inverse
    )
    spectral = 2.0 * jnp.abs(dot3(mean, half) - grid) + jnp.sqrt(sound2) * area
    weight = damping * spectral
    return [flux[v] + weight * third[v] for v in range(5)]


def end_flux(state, prim, third, spacing, speed, area):
    factor = area * lax.rsqrt(dot3(spacing, spacing))
    normal = [s * factor for s in spacing]
    un = dot3(prim, normal)
    q = un - dot3(speed, normal)
    flux = [state[v] * q for v in range(5)]
    for c in range(3):
        flux[1 + c] = flux[1 + c] + prim[3] * normal[c]
    flux[4] = flux[4] + prim[3] * un
    sound = jnp.sqrt(heat_ratio * prim[3] / state[0])
    weight = damping * (jnp.abs(q) + sound * area)
    return [flux[v] + weight * third[v] for v in range(5)]


def kernel(
    sizes,
    flow_ref,
    scale_ref,
    volume_ref,
    surface_ref,
    index_ref,
    table_ref,
    out_ref,
    own_pay,
    cent,
    weights,
    amat,
    bmat,
    hm,
    st,
    pr,
    xs,
    vs,
    sc,
    res,
    halo,
    gr_send,
    gr_recv,
    gt_send,
    gt_recv,
    st_send,
    st_recv,
    sr_send,
    sr_recv,
    ht_send,
    ht_recv,
    hr_send,
    hr_recv,
):
    nt, nr, variables, instances, tc, rc, cen = sizes
    th = lax.axis_index("theta")
    rd = lax.axis_index("rad")
    up, down = lax.rem(th + 1, nt), lax.rem(th + nt - 1, nt)
    lines = tc * rc
    plane = instances * lines
    flow_rows = flow_ref.reshape(variables * plane, LANES)
    halo_rows = halo.reshape(2 * variables * instances * 2 * rc, LANES)
    hub = nt * tc / (2.0 * math.pi)

    barrier = pltpu.get_barrier_semaphore()
    for d in range(1, nr):
        pl.semaphore_signal(
            barrier, inc=1, device_id={"rad": lax.rem(rd + d, nr)}, device_id_type=MESH
        )
    for d in range(1, nt):
        pl.semaphore_signal(
            barrier, inc=1, device_id={"theta": lax.rem(th + d, nt)}, device_id_type=MESH
        )

    per = LANES // (cen * nr)
    offset = (lax.rem(th, per) * nr + rd) * cen
    nodes = surface_ref.shape[1]
    ids = index_ref[...] - (th * nr + rd) * nodes
    chosen = (lax.broadcasted_iota(jnp.int32, (nodes, cen), 0) == ids).astype(jnp.float32)
    placed = (
        lax.broadcasted_iota(jnp.int32, (cen, LANES), 1)
        == lax.broadcasted_iota(jnp.int32, (cen, LANES), 0) + offset
    ).astype(jnp.float32)
    pay = jnp.dot(
        surface_ref[...], chosen, precision=lax.Precision.HIGHEST, preferred_element_type=jnp.float32
    )
    pay = jnp.dot(
        pay, placed, precision=lax.Precision.HIGHEST, preferred_element_type=jnp.float32
    )
    own_pay[rd] = jnp.zeros((16, LANES), jnp.float32)
    own_pay[rd, 0:6] = pay[3:9]
    own_pay[rd, 8:11] = pay[0:3]

    pl.semaphore_wait(barrier, nr - 1 + nt - 1)

    def rad_gather(d):
        peer = lax.rem(rd + d, nr)
        return pltpu.make_async_remote_copy(
            src_ref=own_pay.at[rd],
            dst_ref=own_pay.at[rd],
            send_sem=gr_send.at[d],
            recv_sem=gr_recv.at[d],
            device_id={"rad": peer},
            device_id_type=MESH,
        )

    rad_copies = [rad_gather(d) for d in range(1, nr)]
    for copy in rad_copies:
        copy.start()

    def state_theta(side):
        src = flow_ref.at[:, pl.ds((tc - 2) * rc if side == 0 else 0, 2 * rc), :]
        return pltpu.make_async_remote_copy(
            src_ref=src,
            dst_ref=halo.at[side],
            send_sem=st_send.at[side],
            recv_sem=st_recv.at[side],
            device_id={"theta": up if side == 0 else down},
            device_id_type=MESH,
        )

    theta_copies = [state_theta(0), state_theta(1)]

    def spread(source, base, v, i, j, stride):
        st[v, i, j, 0:instances] = source[pl.ds(base, instances, stride=stride), :]
        st[v, i, j, instances : instances + 1] = source[pl.ds(base, 1), :]

    def own_rows(step, carry):
        v, i = step // tc, step % tc
        for j in range(rc):
            spread(flow_rows, v * plane + i * rc + j, v, i + 2, j + 2, lines)
        return carry

    for copy in rad_copies:
        copy.wait_recv()
    block = own_pay[0]
    for r in range(1, nr):
        block = block + own_pay[r]
    cent[th] = block

    def theta_gather(d):
        peer = lax.rem(th + d, nt)
        return pltpu.make_async_remote_copy(
            src_ref=cent.at[th],
            dst_ref=cent.at[th],
            send_sem=gt_send.at[d],
            recv_sem=gt_recv.at[d],
            device_id={"theta": peer},
            device_id_type=MESH,
        )

    gather_copies = [theta_gather(d) for d in range(1, nt)]
    for copy in gather_copies:
        copy.start()
    for copy in theta_copies:
        copy.start()

    lax.fori_loop(0, variables * tc, own_rows, 0)

    def state_rad(side):
        src = pl.ds(rc, 2) if side == 0 else pl.ds(2, 2)
        dst = pl.ds(0, 2) if side == 0 else pl.ds(rc + 2, 2)
        return pltpu.make_async_remote_copy(
            src_ref=st.at[:, pl.ds(2, tc), src],
            dst_ref=st.at[:, pl.ds(2, tc), dst],
            send_sem=sr_send.at[side],
            recv_sem=sr_recv.at[side],
            device_id={"rad": lax.rem(rd + 1, nr) if side == 0 else lax.rem(rd + nr - 1, nr)},
            device_id_type=MESH,
        )

    rad_states = [state_rad(0), state_rad(1)]

    @pl.when(rd < nr - 1)
    def _():
        rad_states[0].start()

    @pl.when(rd > 0)
    def _():
        rad_states[1].start()

    def primitives(i, j):
        u = [st[v, i, j] for v in range(5)]
        inverse = 1.0 / u[0]
        speed = [u[1 + c] * inverse for c in range(3)]
        for c in range(3):
            pr[c, i, j] = speed[c]
        pr[3, i, j] = (heat_ratio - 1.0) * (u[4] - 0.5 * dot3(u[1:4], speed))

    inner = pl.ds(2, tc)

    def own_prims(j, carry):
        primitives(inner, j + 2)
        for v in range(5):
            res[v, pl.ds(1, tc + 2), j + 2] = jnp.zeros((tc + 2, 8, LANES), jnp.float32)
        return carry

    lax.fori_loop(0, rc, own_prims, 0)
    for j in (1, rc + 2):
        for v in range(5):
            res[v, inner, j] = jnp.zeros((tc, 8, LANES), jnp.float32)

    derivative = derivative_table(instances)

    def temporal(step, carry):
        v, i = step // tc, step % tc
        vol = volume_ref[pl.ds(pl.multiple_of(i * rc, rc), rc), :]
        first = v * plane + i * rc
        parts = [
            vol * flow_rows[pl.ds(pl.multiple_of(first + n * lines, 8), rc), :]
            for n in range(instances)
        ]
        for n in range(instances):
            value = 0.0
            for s in range(1, (instances + 1) // 2):
                value = value + float(derivative[s, 0]) * (
                    parts[(n - s) % instances] - parts[(n + s) % instances]
                )
            out_ref[pl.ds(pl.multiple_of(first + n * lines, 8), rc), :] = value
        return carry

    lax.fori_loop(0, variables * tc, temporal, 0)

    for copy in gather_copies:
        copy.wait_recv()

    blocks = nt // per
    radius8 = (
        lax.broadcasted_iota(jnp.int32, (rc, LANES), 0) + rd * rc
    ).astype(jnp.float32) + (hub + 0.5)
    height = lax.broadcasted_iota(jnp.int32, (LANES, LANES), 0).astype(jnp.float32) + 0.5
    inv_h = 1.0 / support_radius
    for b in range(blocks):
        group = cent[b * per]
        for q in range(1, per):
            group = group + cent[b * per + q]
        cols = slice(b * LANES, (b + 1) * LANES)
        w = group[0:8]
        high = w.astype(jnp.bfloat16)
        low = (w - high.astype(jnp.float32)).astype(jnp.bfloat16)
        weights[:, cols] = jnp.concatenate([high, low], axis=0)
        cx, cy, cz = group[8:9], group[9:10], group[10:11]
        dz = (height - cz) * inv_h
        bmat[:, cols] = dz * dz
        for i in range(tc):
            row = 32 + th * tc + i
            cosine = table_ref[pl.ds(row, 1), :]
            sine = table_ref[pl.ds(row + nt * tc, 1), :]
            dx = (radius8 * cosine - cx) * inv_h
            dy = (radius8 * sine - cy) * inv_h
            amat[i * rc : (i + 1) * rc, cols] = 1.0 + (dx * dx + dy * dy)

    row8 = lax.broadcasted_iota(jnp.int32, (8, LANES), 0)
    width = 2 * LANES
    total = blocks * LANES

    def line_sum(i, j):
        line = i * rc + j
        acc = jnp.zeros((16, LANES), jnp.float32)
        for m in range(0, total, width):
            cols = slice(m, m + width)
            rbf = lax.rsqrt(amat[pl.ds(line, 1), cols] + bmat[:, cols])
            high = rbf.astype(jnp.bfloat16)
            low = (rbf - high.astype(jnp.float32)).astype(jnp.bfloat16)
            for part in (high, low):
                acc = acc + lax.dot_general(
                    weights[:, cols], part, (((1,), (1,)), ((), ())),
                    preferred_element_type=jnp.float32,
                )
        values = acc[0:8] + acc[8:16]
        hm[i + 2, j + 2] = jnp.where(row8 == 6, scale_ref[pl.ds(line, 1), :], values)

    def outer_lines(step, carry):
        line_sum((step // rc) * (tc - 1), step % rc)
        return carry

    lax.fori_loop(0, 2 * rc, outer_lines, 0)

    def geometry_theta(side):
        src = tc + 1 if side == 0 else 2
        dst = 1 if side == 0 else tc + 2
        return pltpu.make_async_remote_copy(
            src_ref=hm.at[src, pl.ds(2, rc)],
            dst_ref=hm.at[dst, pl.ds(2, rc)],
            send_sem=ht_send.at[side],
            recv_sem=ht_recv.at[side],
            device_id={"theta": up if side == 0 else down},
            device_id_type=MESH,
        )

    theta_geometry = [geometry_theta(0), geometry_theta(1)]
    for copy in theta_geometry:
        copy.start()

    def side_lines(step, carry):
        line_sum(1 + step // 2, (step % 2) * (rc - 1))
        return carry

    lax.fori_loop(0, 2 * (tc - 2), side_lines, 0)

    def geometry_rad(side):
        src = rc + 1 if side == 0 else 2
        dst = 1 if side == 0 else rc + 2
        return pltpu.make_async_remote_copy(
            src_ref=hm.at[pl.ds(2, tc), src],
            dst_ref=hm.at[pl.ds(2, tc), dst],
            send_sem=hr_send.at[side],
            recv_sem=hr_recv.at[side],
            device_id={"rad": lax.rem(rd + 1, nr) if side == 0 else lax.rem(rd + nr - 1, nr)},
            device_id_type=MESH,
        )

    rad_geometry = [geometry_rad(0), geometry_rad(1)]

    @pl.when(rd < nr - 1)
    def _():
        rad_geometry[0].start()

    @pl.when(rd > 0)
    def _():
        rad_geometry[1].start()

    def middle_lines(step, carry):
        line_sum(1 + step // (rc - 2), 1 + step % (rc - 2))
        return carry

    lax.fori_loop(0, (tc - 2) * (rc - 2), middle_lines, 0)

    axial = lax.broadcasted_iota(jnp.int32, (8, LANES), 1).astype(jnp.float32) + 0.5

    def geometry(i, j):
        wave = hm[i, j]
        rows = [jnp.broadcast_to(wave[c : c + 1], (8, LANES)) for c in range(7)]
        cell = lax.rem(th * tc + i - 2 + nt * tc, nt * tc)
        radius = (rd * rc + j - 2).astype(jnp.float32) + (hub + 0.5)
        base = (
            radius * table_ref[pl.ds(32 + cell, 1), :],
            radius * table_ref[pl.ds(32 + nt * tc + cell, 1), :],
            axial,
        )
        for c in range(3):
            xs[c, i, j] = base[c] + (rows[c] * table_ref[0:8] + rows[3 + c] * table_ref[8:16])
            vs[c, i, j] = rows[c] * table_ref[16:24] + rows[3 + c] * table_ref[24:32]
        sc[i, j] = rows[6]

    def own_geometry(j, carry):
        for i in range(tc):
            geometry(i + 2, j + 2)
        return carry

    lax.fori_loop(0, rc, own_geometry, 0)

    first = lax.broadcasted_iota(jnp.int32, (tc, 8, LANES), 2) == 0
    last = lax.broadcasted_iota(jnp.int32, (tc, 8, LANES), 2) == LANES - 1

    def before(x):
        return pltpu.roll(x, 1, axis=2)

    def after(x):
        return pltpu.roll(x, LANES - 1, axis=2)

    def axial_faces(step, carry):
        j = step + 2
        right = [st[v, inner, j] for v in range(5)]
        left = [jnp.where(first, x, before(x)) for x in right]
        change = [r - l for r, l in zip(right, left)]
        third = [after(d) - 2.0 * d + jnp.where(first, 0.0, before(d)) for d in change]
        prim_r = [pr[c, inner, j] for c in range(4)]
        prim_l = [jnp.where(first, x, before(x)) for x in prim_r]
        spacing = []
        for c in range(3):
            x = xs[c, inner, j]
            s = x - before(x)
            spacing.append(jnp.where(first, after(s), s))
        speed = [vs[c, inner, j] for c in range(3)]
        speed_sum = [x + jnp.where(first, x, before(x)) for x in speed]
        area = sc[inner, j]
        area_sum = area + jnp.where(first, area, before(area))
        lower = face_flux(left, right, prim_l, prim_r, third, spacing, speed_sum, area_sum)
        end = end_flux(right, prim_r, change, spacing, speed, area)
        for v in range(5):
            res[v, inner, j] += jnp.where(last, end[v], after(lower[v])) - lower[v]
        return carry

    lax.fori_loop(0, rc, axial_faces, 0)

    def faces(cells):
        ll, l, r, rr = cells
        left = [st[(v, *l)] for v in range(5)]
        right = [st[(v, *r)] for v in range(5)]
        third = [
            (st[(v, *rr)] - st[(v, *ll)]) - 3.0 * (right[v] - left[v]) for v in range(5)
        ]
        flux = face_flux(
            left,
            right,
            [pr[(c, *l)] for c in range(4)],
            [pr[(c, *r)] for c in range(4)],
            third,
            [xs[(c, *r)] - xs[(c, *l)] for c in range(3)],
            [vs[(c, *r)] + vs[(c, *l)] for c in range(3)],
            sc[l] + sc[r],
        )
        for v in range(5):
            res[(v, *l)] += flux[v]
            res[(v, *r)] -= flux[v]

    half = rc // 2

    def theta_face(f, part):
        j = pl.ds(2 + part * half, half)
        faces([(f + k, j) for k in range(4)])

    def rad_face(f):
        faces([(inner, f + k) for k in range(4)])

    def theta_inner(step, carry):
        theta_face(2 + step // 2, step % 2)
        return carry

    def rad_inner(step, carry):
        rad_face(2 + step)
        return carry

    lax.fori_loop(0, 2 * (tc - 3), theta_inner, 0)
    lax.fori_loop(0, rc - 3, rad_inner, 0)

    for side in range(2):
        near, far, ghost = (2, 3, 1) if side == 0 else (rc + 1, rc, rc + 2)
        ghost2 = 0 if side == 0 else rc + 3
        at_end = (rd == 0) if side == 0 else (rd == nr - 1)

        @pl.when(at_end)
        def _():
            for v in range(5):
                value = st[v, inner, near]
                st[v, inner, ghost] = value
                st[v, inner, ghost2] = value
            for c in range(3):
                xs[c, inner, ghost] = 2.0 * xs[c, inner, near] - xs[c, inner, far]
                vs[c, inner, ghost] = vs[c, inner, near]
            sc[inner, ghost] = sc[inner, near]

        @pl.when(jnp.logical_not(at_end))
        def _():
            rad_states[side].wait_recv()
            rad_geometry[side].wait_recv()
            for i in range(tc):
                geometry(i + 2, ghost)

        primitives(inner, ghost)

    def rad_outer(step, carry):
        rad_face(step + (rc - 3) * (step // 2))
        return carry

    lax.fori_loop(0, 4, rad_outer, 0)

    for side in range(2):
        theta_geometry[side].wait_recv()
        theta_copies[side].wait_recv()

    def ghost_cells(step, carry):
        side, j = step // rc, step % rc
        for v in range(variables):
            for layer in range(2):
                start = ((side * variables + v) * instances * 2 + layer) * rc + j
                spread(halo_rows, start, v, side * (tc + 2) + layer, j + 2, 2 * rc)
        ghost = 1 + side * (tc + 1)
        geometry(ghost, j + 2)
        primitives(ghost, j + 2)
        return carry

    lax.fori_loop(0, 2 * rc, ghost_cells, 0)

    def theta_outer(step, carry):
        f = step // 2
        theta_face(f + (tc - 3) * (f // 2), step % 2)
        return carry

    lax.fori_loop(0, 8, theta_outer, 0)

    def finish(step, carry):
        v, i = step // tc, step % tc
        for j in range(rc):
            rows = pl.ds(v * plane + i * rc + j, instances, stride=lines)
            out_ref[rows, :] = out_ref[rows, :] + res[v, i + 2, j + 2, 0:instances]
        return carry

    lax.fori_loop(0, variables * tc, finish, 0)

    for copy in rad_copies + gather_copies + theta_copies + theta_geometry:
        copy.wait_send()

    @pl.when(rd < nr - 1)
    def _():
        rad_states[0].wait_send()
        rad_geometry[0].wait_send()

    @pl.when(rd > 0)
    def _():
        rad_states[1].wait_send()
        rad_geometry[1].wait_send()


def on_device(nt, nr, flow_state, face_scale, volume, surface, centre_index):
    variables, instances, tc, rc, na = flow_state.shape
    cen = centre_index.shape[0]
    sizes = (nt, nr, variables, instances, tc, rc, cen)
    table = jnp.asarray(constant_rows(instances, nt * tc))
    total = cen * nt * nr
    vmem = pl.BlockSpec(memory_space=pltpu.VMEM)
    f32 = jnp.float32
    cells = (tc + 4, rc + 4, 8, LANES)
    out = pl.pallas_call(
        functools.partial(kernel, sizes),
        out_shape=jax.ShapeDtypeStruct((variables * instances * tc * rc, na), f32),
        in_specs=[vmem] * 6,
        out_specs=vmem,
        scratch_shapes=[
            pltpu.VMEM((nr, 16, LANES), f32),
            pltpu.VMEM((nt, 16, LANES), f32),
            pltpu.VMEM((16, total), jnp.bfloat16),
            pltpu.VMEM((tc * rc, total), f32),
            pltpu.VMEM((LANES, total), f32),
            pltpu.VMEM(cells, f32),
            pltpu.VMEM((5,) + cells, f32),
            pltpu.VMEM((4,) + cells, f32),
            pltpu.VMEM((3,) + cells, f32),
            pltpu.VMEM((3,) + cells, f32),
            pltpu.VMEM(cells, f32),
            pltpu.VMEM((5,) + cells, f32),
            pltpu.VMEM((2, variables * instances, 2 * rc, LANES), f32),
            pltpu.SemaphoreType.DMA((nr,)),
            pltpu.SemaphoreType.DMA((nr,)),
            pltpu.SemaphoreType.DMA((nt,)),
            pltpu.SemaphoreType.DMA((nt,)),
        ]
        + [pltpu.SemaphoreType.DMA((2,))] * 8,
        compiler_params=pltpu.CompilerParams(
            collective_id=0, has_side_effects=True, vmem_limit_bytes=40 * 1024 * 1024
        ),
    )(
        flow_state.reshape(variables * instances, tc * rc, na),
        face_scale.reshape(tc * rc, na),
        volume.reshape(tc * rc, na),
        surface,
        centre_index.reshape(1, cen),
        table,
    )
    return out.reshape(flow_state.shape)


def solution(mesh):
    return jax.shard_map(
        functools.partial(on_device, mesh.shape["theta"], mesh.shape["rad"]),
        mesh=mesh,
        in_specs=(
            P(None, None, "theta", "rad", None),
            P("theta", "rad", None),
            P("theta", "rad", None),
            P(None, ("theta", "rad")),
            P(("theta", "rad")),
        ),
        out_specs=P(None, None, "theta", "rad", None),
        check_vma=False,
    )
```

time: 114 us -> 37.3 us (0.33)
  the two profiles are of different devices: /device:TPU:0 before, /device:TPU:8 now
where the time goes in v1:
time: 37.3 us; the launch traced here: 36.9 us
  Pallas kernels  31.4 us (84%)
  local copies, waits for them, and re-layouts  5.45 us (15%)
    pallas_call x1, Pallas kernels, on_device(): pl.pallas_call(functools.partial(kernel, sizes), out_shape=jax.ShapeDtype...  31.4 us
    unnamed x13, local copies, waits for them, and re-layouts  5.45 us

profile of v1, /device:TPU:8, one launch (start us, length us, event | category | flops | bytes accessed | tf_op | source)
XLA Modules:
  0.0 36.9 jit_solution(17028594654305500350)
XLA Ops:
  0.0 0.0 copy-start.5
  0.0 0.7 %copy-done.5 = s32[32]{0:T(128)S(1)} copy-done((s32[32]{0:T(128)S(1)}, s32[32]{0:T(128)}, u32[]{:S(2)}) %copy-start.5) | copy-done | bytes 152
  0.7 0.0 copy-start
  0.7 1.1 %copy-done = f32[5,7,4,8,128]{4,3,2,1,0:T(8,128)S(1)} copy-done((f32[5,7,4,8,128]{4,3,2,1,0:T(8,128)S(1)}, f32[5,7,4,8,128]{4,3,2,1,0:T(8,128)}, u32[]{:S(2)}) %copy-start) | copy-done | bytes 573464
  1.7 0.0 copy-start.1
  1.7 0.8 %copy-done.1 = f32[96,128]{1,0:T(8,128)S(1)} copy-done((f32[96,128]{1,0:T(8,128)S(1)}, f32[96,128]{1,0:T(8,128)}, u32[]{:S(2)}) %copy-start.1) | copy-done | bytes 49176
  2.5 0.0 copy-start.2
  2.5 0.7 %copy-done.2 = f32[4,8,128]{2,1,0:T(8,128)S(1)} copy-done((f32[4,8,128]{2,1,0:T(8,128)S(1)}, f32[4,8,128]{2,1,0:T(8,128)}, u32[]{:S(2)}) %copy-start.2) | copy-done | bytes 16408
  3.2 0.0 copy-start.3
  3.2 0.7 %copy-done.3 = f32[4,8,128]{2,1,0:T(8,128)S(1)} copy-done((f32[4,8,128]{2,1,0:T(8,128)S(1)}, f32[4,8,128]{2,1,0:T(8,128)}, u32[]{:S(2)}) %copy-start.3) | copy-done | bytes 16408
  4.0 0.0 copy-start.4
  4.0 0.7 %copy-done.4 = f32[9,64]{1,0:T(8,128)S(1)} copy-done((f32[9,64]{1,0:T(8,128)S(1)}, f32[9,64]{1,0:T(8,128)}, u32[]{:S(2)}) %copy-start.4) | copy-done | bytes 2328
  4.6 31.4 %shard_map.64 = f32[1120,128]{1,0:T(8,128)S(1)} custom-call(f32[35,32,128]{2,1,0:T(8,128)S(1)} %bitcast.6, f32[32,128]{1,0:T(8,128)S(1)} %bitcast.7, f32[32,128]{1,0:T(8,128)S(1)} %bitcast.8, f32[9,64]{1,0:T(8,128)S(1)} %copy-done.4, s32[1,32]{1,0:T(1,128)S(1)} %bitcast.9, f32[96,128]{1,0:T(8,128)S(1)} %copy-done.1), custom_call_target="tpu_custom_call" | custom-call | tf_op jit(solution)/shard_map/pallas_call | solution.py:584
  36.1 0.8 %copy.8 = f32[5,7,4,8,128]{4,3,2,1,0:T(8,128)} copy(f32[5,7,4,8,128]{4,3,2,1,0:T(8,128)S(1)} %bitcast.5) | data formatting | bytes 1146880
Async XLA Ops:
  0.0 0.7 %copy-start.5 = (s32[32]{0:T(128)S(1)}, s32[32]{0:T(128)}, u32[]{:S(2)}) copy-start(s32[32]{0:T(128)} %param.10) | copy-start | bytes 388
  0.7 1.1 %copy-start = (f32[5,7,4,8,128]{4,3,2,1,0:T(8,128)S(1)}, f32[5,7,4,8,128]{4,3,2,1,0:T(8,128)}, u32[]{:S(2)}) copy-start(f32[5,7,4,8,128]{4,3,2,1,0:T(8,128)} %param.6) | copy-start | bytes 1720324
  1.7 0.8 %copy-start.1 = (f32[96,128]{1,0:T(8,128)S(1)}, f32[96,128]{1,0:T(8,128)}, u32[]{:S(2)}) copy-start(f32[96,128]{1,0:T(8,128)} %constant.2.clone.table_ref) | copy-start | bytes 147460
  2.5 0.7 %copy-start.2 = (f32[4,8,128]{2,1,0:T(8,128)S(1)}, f32[4,8,128]{2,1,0:T(8,128)}, u32[]{:S(2)}) copy-start(f32[4,8,128]{2,1,0:T(8,128)} %param.7) | copy-start | bytes 49156
  3.2 0.7 %copy-start.3 = (f32[4,8,128]{2,1,0:T(8,128)S(1)}, f32[4,8,128]{2,1,0:T(8,128)}, u32[]{:S(2)}) copy-start(f32[4,8,128]{2,1,0:T(8,128)} %param.8) | copy-start | bytes 49156
  4.0 0.7 %copy-start.4 = (f32[9,64]{1,0:T(8,128)S(1)}, f32[9,64]{1,0:T(8,128)}, u32[]{:S(2)}) copy-start(f32[9,64]{1,0:T(8,128)} %surface_ref.1) | copy-start | bytes 6916

commit v2 on v1

--- a/solution.py
+++ b/solution.py
@@ -88,13 +88,19 @@
 
 def kernel(
     sizes,
+    flow_in,
+    scale_in,
+    volume_in,
+    surface_in,
+    index_in,
+    table_in,
+    out_ref,
     flow_ref,
     scale_ref,
     volume_ref,
     surface_ref,
     index_ref,
     table_ref,
-    out_ref,
     own_pay,
     cent,
     weights,
@@ -120,6 +126,7 @@
     ht_recv,
     hr_send,
     hr_recv,
+    in_sem,
 ):
     nt, nr, variables, instances, tc, rc, cen = sizes
     th = lax.axis_index("theta")
@@ -131,6 +138,21 @@
     halo_rows = halo.reshape(2 * variables * instances * 2 * rc, LANES)
     hub = nt * tc / (2.0 * math.pi)
 
+    inputs = [
+        pltpu.make_async_copy(src, dst, in_sem.at[k])
+        for k, (src, dst) in enumerate(
+            (
+                (surface_in, surface_ref),
+                (index_in, index_ref),
+                (flow_in, flow_ref),
+                (volume_in, volume_ref),
+                (table_in, table_ref),
+                (scale_in, scale_ref),
+            )
+        )
+    ]
+    for copy in inputs:
+        copy.start()
     barrier = pltpu.get_barrier_semaphore()
     for d in range(1, nr):
         pl.semaphore_signal(
@@ -140,6 +162,9 @@
         pl.semaphore_signal(
             barrier, inc=1, device_id={"theta": lax.rem(th + d, nt)}, device_id_type=MESH
         )
+
+    for copy in inputs[:2]:
+        copy.wait()
 
     per = LANES // (cen * nr)
     offset = (lax.rem(th, per) * nr + rd) * cen
@@ -200,6 +225,8 @@
             spread(flow_rows, v * plane + i * rc + j, v, i + 2, j + 2, lines)
         return carry
 
+    for copy in inputs[2:]:
+        copy.wait()
     for copy in rad_copies:
         copy.wait_recv()
     block = own_pay[0]
@@ -584,9 +611,15 @@
     out = pl.pallas_call(
         functools.partial(kernel, sizes),
         out_shape=jax.ShapeDtypeStruct((variables * instances * tc * rc, na), f32),
-        in_specs=[vmem] * 6,
+        in_specs=[pl.BlockSpec(memory_space=pltpu.HBM)] * 6,
         out_specs=vmem,
         scratch_shapes=[
+            pltpu.VMEM((variables * instances, tc * rc, na), f32),
+            pltpu.VMEM((tc * rc, na), f32),
+            pltpu.VMEM((tc * rc, na), f32),
+            pltpu.VMEM(surface.shape, f32),
+            pltpu.VMEM((1, cen), jnp.int32),
+            pltpu.VMEM(table.shape, f32),
             pltpu.VMEM((nr, 16, LANES), f32),
             pltpu.VMEM((nt, 16, LANES), f32),
             pltpu.VMEM((16, total), jnp.bfloat16),
@@ -605,9 +638,10 @@
             pltpu.SemaphoreType.DMA((nt,)),
             pltpu.SemaphoreType.DMA((nt,)),
         ]
-        + [pltpu.SemaphoreType.DMA((2,))] * 8,
+        + [pltpu.SemaphoreType.DMA((2,))] * 8
+        + [pltpu.SemaphoreType.DMA((6,))],
         compiler_params=pltpu.CompilerParams(
-            collective_id=0, has_side_effects=True, vmem_limit_bytes=40 * 1024 * 1024
+            collective_id=0, has_side_effects=True, vmem_limit_bytes=64 * 1024 * 1024
         ),
     )(
         flow_state.reshape(variables * instances, tc * rc, na),

time: 37.3 us -> 30.7 us (0.82)
  the two profiles are of different devices: /device:TPU:8 before, /device:TPU:0 now
where the time goes in v2:
time: 30.7 us; the launch traced here: 30.5 us
  Pallas kernels  28.6 us (93%)
  local copies, waits for them, and re-layouts  1.91 us (6%)
    pallas_call x1, Pallas kernels, on_device(): pl.pallas_call(functools.partial(kernel, sizes), out_shape=jax.ShapeDtype...  28.6 us
    unnamed x1, local copies, waits for them, and re-layouts  1.91 us

profile of v2, /device:TPU:0, one launch (start us, length us, event | category | flops | bytes accessed | tf_op | source)
XLA Modules:
  0.0 30.5 jit_solution(5080060300787364218)
XLA Ops:
  0.0 28.6 %shard_map.64 = f32[1120,128]{1,0:T(8,128)} custom-call(f32[35,32,128]{2,1,0:T(8,128)} %bitcast.6, f32[32,128]{1,0:T(8,128)} %bitcast.7, f32[32,128]{1,0:T(8,128)} %bitcast.8, f32[9,64]{1,0:T(8,128)} %surface_in.1, s32[1,32]{1,0:T(1,128)} %bitcast.9, f32[96,128]{1,0:T(8,128)} %constant.2.clone.table_in), custom_call_target="tpu_custom_call" | custom-call | tf_op jit(solution)/shard_map/pallas_call | solution.py:611
  28.6 1.9 %copy.8 = f32[5,7,4,8,128]{4,3,2,1,0:T(8,128)} copy(f32[5,7,4,8,128]{4,3,2,1,0:T(8,128)} %bitcast.5) | data formatting | bytes 1146880

commit v3 on v2

--- a/solution.py
+++ b/solution.py
@@ -554,36 +554,43 @@
 
     for side in range(2):
         theta_geometry[side].wait_recv()
+
+    def ghost_geometry(step, carry):
+        geometry(1 + (step // rc) * (tc + 1), step % rc + 2)
+        return carry
+
+    lax.fori_loop(0, 2 * rc, ghost_geometry, 0)
+
+    for side in range(2):
         theta_copies[side].wait_recv()
-
-    def ghost_cells(step, carry):
-        side, j = step // rc, step % rc
-        for v in range(variables):
-            for layer in range(2):
-                start = ((side * variables + v) * instances * 2 + layer) * rc + j
-                spread(halo_rows, start, v, side * (tc + 2) + layer, j + 2, 2 * rc)
         ghost = 1 + side * (tc + 1)
-        geometry(ghost, j + 2)
-        primitives(ghost, j + 2)
-        return carry
-
-    lax.fori_loop(0, 2 * rc, ghost_cells, 0)
-
-    def theta_outer(step, carry):
-        f = step // 2
-        theta_face(f + (tc - 3) * (f // 2), step % 2)
-        return carry
-
-    lax.fori_loop(0, 8, theta_outer, 0)
-
-    def finish(step, carry):
-        v, i = step // tc, step % tc
-        for j in range(rc):
-            rows = pl.ds(v * plane + i * rc + j, instances, stride=lines)
-            out_ref[rows, :] = out_ref[rows, :] + res[v, i + 2, j + 2, 0:instances]
-        return carry
-
-    lax.fori_loop(0, variables * tc, finish, 0)
+        early = tc // 2
+
+        def ghost_cells(j, carry):
+            for v in range(variables):
+                for layer in range(2):
+                    start = ((side * variables + v) * instances * 2 + layer) * rc + j
+                    spread(halo_rows, start, v, side * (tc + 2) + layer, j + 2, 2 * rc)
+            return carry
+
+        lax.fori_loop(0, rc, ghost_cells, 0)
+        for part in range(2):
+            primitives(ghost, pl.ds(2 + part * half, half))
+
+        def theta_outer(step, carry):
+            theta_face(side * (tc - 1) + step // 2, step % 2)
+            return carry
+
+        lax.fori_loop(0, 4, theta_outer, 0)
+
+        def finish(step, carry):
+            v, i = step // early, side * early + step % early
+            for j in range(rc):
+                rows = pl.ds(v * plane + i * rc + j, instances, stride=lines)
+                out_ref[rows, :] = out_ref[rows, :] + res[v, i + 2, j + 2, 0:instances]
+            return carry
+
+        lax.fori_loop(0, variables * early, finish, 0)
 
     for copy in rad_copies + gather_copies + theta_copies + theta_geometry:
         copy.wait_send()

time: 30.7 us -> 30.7 us (level)
  no operation moved by 1% of the time
where the time goes in v3:
time: 30.7 us; the launch traced here: 30.5 us
  Pallas kernels  28.6 us (93%)
  local copies, waits for them, and re-layouts  1.91 us (6%)
    pallas_call x1, Pallas kernels, on_device(): pl.pallas_call(functools.partial(kernel, sizes), out_shape=jax.ShapeDtype...  28.6 us
    unnamed x1, local copies, waits for them, and re-layouts  1.91 us

profile of v3, /device:TPU:0, one launch (start us, length us, event | category | flops | bytes accessed | tf_op | source)
XLA Modules:
  0.0 30.5 jit_solution(14221380320997836460)
XLA Ops:
  0.0 28.6 %shard_map.64 = f32[1120,128]{1,0:T(8,128)} custom-call(f32[35,32,128]{2,1,0:T(8,128)} %bitcast.6, f32[32,128]{1,0:T(8,128)} %bitcast.7, f32[32,128]{1,0:T(8,128)} %bitcast.8, f32[9,64]{1,0:T(8,128)} %surface_in.1, s32[1,32]{1,0:T(1,128)} %bitcast.9, f32[96,128]{1,0:T(8,128)} %constant.2.clone.table_in), custom_call_target="tpu_custom_call" | custom-call | tf_op jit(solution)/shard_map/pallas_call | solution.py:618
  28.6 1.9 %copy.8 = f32[5,7,4,8,128]{4,3,2,1,0:T(8,128)} copy(f32[5,7,4,8,128]{4,3,2,1,0:T(8,128)} %bitcast.5) | data formatting | bytes 1146880
